TPU v7x, 32 devices: a whole 2x2x4 slice. The times are simulated.
32 devices in a mesh: blk: 16 (over z, y, core), mpo: 2 (over x).
Axes of the slice: x: 2, y: 2, z: 4, core: 2. Of those that a mesh axis runs over, the one named last changes fastest.
Arguments:
- wave: bfloat16 [1536, 128, 128], P('blk'), may hold values from -6 to 6
- left_env: bfloat16 [2, 64, 128, 128], P('mpo', 'blk'), may hold values from -0.5 to 0.5
- right_env: bfloat16 [2, 64, 128, 128], P('mpo', 'blk'), may hold values from -0.375 to 0.375
- right_sector: int32 [1536, 1], P('blk'), may hold values from 0 to 63; in each aligned block of 96 rows (0 to 95, 96 to 191, ...) at most 2 rows name the same one
- right_home: int32 [64], replicated, may hold values from 0 to 63, each once
Outputs:
- product: bfloat16 [1536, 128, 128], P('blk', None, 'mpo')
Inputs may be any that keep to these rules, and one draw needn't show every extreme that they name: `right_sector`: among the 96 blocks of one device (aligned blocks of rows) no right sector appears more than 2 times, and some sector appears exactly 2 times; every sector appears somewhere. `right_home`: each sector has its own storage row.
All inputs are finite; a program needn't handle non-finite values.
Results may differ from a plain program's by a relative error of at most 0.008.
Values may be sent and summed in bfloat16 or wider, within the bound.
A program may use at most 64 MiB of HBM per device.

v0:
```python
import jax
import jax.numpy as jnp
from jax import lax
from jax.sharding import PartitionSpec as P


def local(wave, left_env, right_env, right_sector, right_home):
    blocks = wave.shape[0]
    sectors = left_env.shape[1]
    local_left = jnp.arange(blocks, dtype=jnp.int32) * sectors // blocks
    places = jnp.take(right_home, right_sector[:, 0], axis=0)
    chosen = jnp.take(left_env[0], local_left, axis=0)
    left = jnp.einsum("bik,bkj->bij", chosen, wave, preferred_element_type=jnp.float32).astype(
        jnp.bfloat16
    )
    every_right = lax.all_gather(right_env[0], "blk", axis=0, tiled=True)
    picked = jnp.take(every_right, places, axis=0)
    terms = jnp.einsum("bik,bjk->bij", left, picked, preferred_element_type=jnp.float32)
    summed = lax.psum_scatter(terms, "mpo", scatter_dimension=2, tiled=True)
    return summed.astype(jnp.bfloat16)


def solution(mesh):
    in_specs = (
        P("blk", None, None),
        P("mpo", "blk", None, None),
        P("mpo", "blk", None, None),
        P("blk", None),
        P(),
    )
    out_specs = P("blk", None, "mpo")
    return jax.shard_map(local, mesh=mesh, in_specs=in_specs, out_specs=out_specs, check_vma=False)
```

profile of v0, /device:TPU:0, one launch (start us, length us, event | category | flops | bytes accessed | tf_op | source)
XLA Modules:
  0.0 152.9 jit_solution(2068127351979968424)
XLA Ops:
  6.5 0.0 copy-start
  6.5 0.0 all-gather.3.cloned.1.call-start
  6.5 0.7 all-gather.3.cloned.1.call-update
  7.3 0.0 reduce-scatter.2.cloned.1.call-start
  7.3 0.8 fusion.16
  8.1 1.6 %gather_fusion.1 = s32[96]{0:T(128)S(1)} fusion(s32[64]{0:T(128)} %param.9, s32[1024]{0:T(1024)S(1)} %pad_clamp_fusion.1), kind=kCustom, calls=%fused_computation.1 | custom fusion | bytes 1152 | tf_op jit(solution)/shard_map/jit(_take)/gather | solution.py:11
  9.8 0.0 copy-start.1
  9.8 3.6 %gather_fusion = bf16[96,128,128]{2,1,0:T(8,128)(2,1)} fusion(bf16[4,128,128]{2,1,0:T(8,128)(2,1)} %bitcast.16, s32[1024]{0:T(1024)S(1)} %pad_clamp_fusion.2), kind=kCustom, calls=%fused_computation | custom fusion | bytes 6291840 | tf_op jit(solution)/shard_map/jit(_take)/gather | solution.py:12
  13.4 0.0 copy-done.1
  13.5 40.2 %all-gather.3.cloned.1.call-done = bf16[1,64,128,128]{3,2,0,1:T(8,128)(2,1)} async-done(((bf16[1,4,128,128]{3,2,0,1:T(8,128)(2,1)}), bf16[1,64,128,128]{3,2,0,1:T(8,128)(2,1)}) %all-gather.3.cloned.1.call-update) | async-done | bytes 2097168 | tf_op jit(solution)/shard_map/all_gather | solution.py:16
  53.7 4.3 %gather_fusion.2 = bf16[96,128,128]{2,1,0:T(8,128)(2,1)} fusion(bf16[64,128,128]{2,1,0:T(8,128)(2,1)} %bitcast.17, s32[1024]{0:T(1024)S(1)} %pad_clamp_fusion), kind=kCustom, calls=%fused_computation.2 | custom fusion | bytes 6291840 | tf_op jit(solution)/shard_map/jit(_take)/gather | solution.py:17
  58.0 0.0 copy-done
  58.0 8.7 %fusion = f32[96,128,128]{1,2,0:T(8,128)} fusion(bf16[96,128,128]{2,1,0:T(8,128)(2,1)} %gather_fusion.2, pred[96]{0:T(512)(128)(4,1)S(1)} %get-tuple-element.5, bf16[96,128,128]{2,1,0:T(8,128)(2,1)S(1)} %copy-done, bf16[96,128,128]{2,1,0:T(8,128)(2,1)} %gather_fusion, pred[96]{0:T(512)(128)(4,1)S(1)} %compare_and_fusion), kind=kOutput, calls=%fused_computation.3 | convolution fusion | flops 810024960 | bytes 15728832 | tf_op jit(solution)/shard_map/bik,bjk->bij/dot_general | solution.py:18
  66.7 0.0 reduce-scatter.2.cloned.1.call-update
  66.7 76.0 %reduce-scatter.2.cloned.1.call-done = f32[96,128,64]{1,2,0:T(8,128)} async-done(((f32[96,128,128]{1,2,0:T(8,128)}), f32[96,128,64]{1,2,0:T(8,128)}) %reduce-scatter.2.cloned.1.call-update) | async-done | bytes 3145744 | tf_op jit(solution)/shard_map/reduce_scatter | solution.py:19
  142.7 3.4 %convert_element_type.7 = bf16[96,128,64]{1,2,0:T(8,128)(2,1)} convert(f32[96,128,64]{1,2,0:T(8,128)} %reduce-scatter.2.cloned.1.call-done) | non-fusion elementwise | flops 786432 | bytes 4718592 | tf_op jit(solution)/shard_map/convert_element_type | solution.py:20
  (6 shorter events, 0.1 us)
Async XLA Ops:
  6.5 51.5 %copy-start = (bf16[96,128,128]{2,1,0:T(8,128)(2,1)S(1)}, bf16[96,128,128]{2,1,0:T(8,128)(2,1)}, u32[]{:S(2)}) copy-start(bf16[96,128,128]{2,1,0:T(8,128)(2,1)} %param.5) | copy-start | bytes 9437188
  6.5 47.1 %all-gather.3.cloned.1.call-start = ((), (), s32[]{:S(2)}) async-start(), calls=%async_computation.2 | async-start | bytes 2228224 | tf_op jit(solution)/shard_map/all_gather | solution.py:16
  7.3 135.4 %reduce-scatter.2.cloned.1.call-start = ((), (), s32[]{:S(2)}) async-start(), calls=%async_computation.1 | async-start | bytes 9437184 | tf_op jit(solution)/shard_map/reduce_scatter | solution.py:19
  9.8 3.6 %copy-start.1 = (s32[96,1]{0,1:T(1,128)S(1)}, s32[96,1]{0,1:T(1,128)}, u32[]{:S(2)}) copy-start(s32[96,1]{0,1:T(1,128)} %param.8) | copy-start | bytes 1156
Sparse Core Ops, SparseCore 0:
  9.5 44.0 all-gather.2
  66.8 75.8 reduce-scatter.1
where the time goes:
time: 153 us
  waiting for transfers between devices  117 us (76%)
  between operations  13.4 us (9%)
  local copies, waits for them, and re-layouts  9.55 us (6%)
  matrix products  8.7 us (6%)
  other arithmetic  4.28 us (3%)
    reduce_scatter x1, waiting for transfers between devices, local(): summed = lax.psum_scatter(terms, 'mpo', scatter_dimension=2, tiled=True)  76 us
    all_gather x1, waiting for transfers between devices, local(): every_right = lax.all_gather(right_env[0], 'blk', axis=0, tiled=True)  40.2 us
    dot_general x1, matrix products, local(): jnp.einsum('bik,bjk->bij', left, picked, preferred_element_type=jnp.float32)  8.7 us
    gather x1, local copies, waits for them, and re-layouts, local(): picked = jnp.take(every_right, places, axis=0)  4.34 us
    gather x1, local copies, waits for them, and re-layouts, local(): chosen = jnp.take(left_env[0], local_left, axis=0)  3.62 us
    convert_element_type x1, other arithmetic, local(): return summed.astype(jnp.bfloat16)  3.39 us
  transfers between devices with their start and end apart: 2, of which 2 were waited for; matrix products, arithmetic and copies ran while one was open for 4% of the time, Pallas kernels for 0%

commit v1 on v0

v1 whole, which is shorter than its diff:
```python
import functools

import jax
import jax.numpy as jnp
from jax import lax
from jax.experimental import pallas as pl
from jax.experimental.pallas import tpu as pltpu
from jax.sharding import PartitionSpec as P

MESH = pl.DeviceIdType.MESH
PIECES = 4


def kernel(
    sizes, sector, home, wave, lenv, renv, out,
    rights, lefts, blocks_in, left, result,
    wave_sem, own_sem, x_send, x_recv, l_send, l_recv, z_send, y_send, c_send, recv, out_sem,
):
    lines, terms, chunks = sizes
    count, rows, cols = blocks_in.shape
    held, part = rights.shape[2], rights.shape[3]
    per = terms // chunks
    piece = count // PIECES
    b, m = lax.axis_index("blk"), lax.axis_index("mpo")
    z, y, c = b // 4, (b // 2) % 2, b % 2

    def at(zz, yy, cc):
        return zz * 4 + yy * 2 + cc

    sibling, across = at(z, y, 1 - c), at(z, 1 - y, c)
    peers = [lax.rem(m + d, terms) for d in range(1, terms)]

    def rows_of(term):
        return renv.at[0, :, pl.ds(pl.multiple_of(term * part, part), part), :]

    own_right = pltpu.make_async_copy(rows_of(m), rights.at[b, m], own_sem.at[0])
    own_left = pltpu.make_async_copy(lenv.at[0], lefts.at[:, m], own_sem.at[1])
    loads = [
        pltpu.make_async_copy(
            wave.at[pl.ds(i * piece, piece)], blocks_in.at[pl.ds(i * piece, piece)], wave_sem.at[i]
        )
        for i in range(PIECES)
    ]
    own_right.start()

    barrier = pltpu.get_barrier_semaphore()

    def greet(**where):
        pl.semaphore_signal(barrier, inc=1, device_id=where, device_id_type=MESH)

    for peer in peers:
        greet(mpo=peer)
    greet(blk=across)
    greet(blk=sibling)

    @pl.when(z > 0)
    def _():
        greet(blk=b - 4)

    @pl.when(z < lines - 1)
    def _():
        greet(blk=b + 4)

    own_left.start()
    for load in loads:
        load.start()
    least = jnp.where(z > 0, 1, 0) + jnp.where(z < lines - 1, 1, 0)
    pl.semaphore_wait(barrier, least + 2 + len(peers))

    x_copies = [
        pltpu.make_async_remote_copy(
            rows_of(peer), rights.at[b, m], x_send.at[i], x_recv.at[m],
            device_id={"mpo": peer}, device_id_type=MESH,
        )
        for i, peer in enumerate(peers)
    ]
    l_copies = [
        pltpu.make_async_remote_copy(
            lenv.at[0], lefts.at[:, m], l_send.at[i], l_recv.at[m],
            device_id={"mpo": peer}, device_id_type=MESH,
        )
        for i, peer in enumerate(peers)
    ]
    for copy in x_copies:
        copy.start()
    for copy in l_copies:
        copy.start()

    def unit(bb, q):
        return rights.at[bb, pl.ds(q * per, per)]

    def to(bb, q, sem, target):
        return pltpu.make_async_remote_copy(
            unit(bb, q), unit(bb, q), sem, recv.at[bb, q],
            device_id={"blk": target}, device_id_type=MESH,
        )

    def up(zz, q):
        return to(at(zz, y, c), q, z_send.at[0, zz, q], b + 4)

    def down(zz, q):
        return to(at(zz, y, c), q, z_send.at[1, zz, q], b - 4)

    def over(zz, q):
        return to(at(zz, y, c), q, y_send.at[zz, q], across)

    def beside(bb, q):
        return to(bb, q, c_send.at[bb, q], sibling)

    def spread(zz, q, upward, downward):
        if upward:

            @pl.when(z < lines - 1)
            def _():
                up(zz, q).start()

        if downward:

            @pl.when(z > 0)
            def _():
                down(zz, q).start()

        over(zz, q).start()
        beside(at(zz, y, c), q).start()

    order = [m, 1 - m] if chunks == 2 else [0]

    def wait_x(peer):
        pltpu.make_async_copy(rows_of(peer), rights.at[b, peer], x_recv.at[peer]).wait()

    def own_line():
        own_right.wait()
        if chunks == 2:
            spread(z, m, True, True)
        for peer in peers:
            wait_x(peer)
        if chunks == 2:
            spread(z, 1 - m, True, True)
        else:
            spread(z, 0, True, True)

    def hop(h):
        for q in order:

            @pl.when(z >= h)
            def _():
                beside(at(z - h, y, c), q).wait_recv()
                spread(z - h, q, True, False)

            @pl.when(z + h < lines)
            def _():
                beside(at(z + h, y, c), q).wait_recv()
                spread(z + h, q, False, True)

    def cross(h):
        for q in order:

            @pl.when(z >= h)
            def _():
                bb = at(z - h, 1 - y, c)
                beside(bb, q).wait_recv()
                beside(bb, q).start()

            if h > 0:

                @pl.when(z + h < lines)
                def _():
                    bb = at(z + h, 1 - y, c)
                    beside(bb, q).wait_recv()
                    beside(bb, q).start()

    def first(i):
        loads[i].wait()

        def body(t, carry):
            j = i * piece + 2 * t
            a = j * held // count
            stack = jnp.concatenate([lefts[a, w] for w in range(terms)], axis=0)
            pair = jnp.concatenate([blocks_in[j], blocks_in[j + 1]], axis=1)
            both = jnp.dot(stack, pair, preferred_element_type=jnp.float32).astype(jnp.bfloat16)
            for w in range(terms):
                left[j, w] = both[w * rows:(w + 1) * rows, :cols]
                left[j + 1, w] = both[w * rows:(w + 1) * rows, cols:]
            return carry

        lax.fori_loop(0, piece // 2, body, 0)

    own_line()
    own_left.wait()
    for peer in peers:
        pltpu.make_async_copy(lenv.at[0], lefts.at[:, peer], l_recv.at[peer]).wait()
    first(0)
    for h in range(1, lines):
        hop(h)
        cross(h - 1)
        if h < PIECES - 1:
            first(h)
    cross(lines - 1)
    for i in range(min(lines, PIECES - 1), PIECES):
        first(i)

    def each(body):
        def step(zz, carry):
            for q in range(chunks):
                body(zz, q)
            return carry

        lax.fori_loop(0, lines, step, 0)

    def arrived(zz, q):
        for yy in range(2):
            beside(at(zz, yy, 1 - c), q).wait_recv()

    each(arrived)

    stores = []
    for i in range(PIECES):

        def second(j, carry):
            place = home[sector[j, 0]]
            source, slot = place // held, place % held
            mine = jnp.concatenate([left[j, w] for w in range(terms)], axis=1)
            right = jnp.concatenate([rights[source, w, slot] for w in range(terms)], axis=1)
            result[j] = lax.dot_general(
                mine, right, (((1,), (1,)), ((), ())), preferred_element_type=jnp.float32
            ).astype(jnp.bfloat16)
            return carry

        lax.fori_loop(i * piece, (i + 1) * piece, second, 0, unroll=4)
        store = pltpu.make_async_copy(
            result.at[pl.ds(i * piece, piece)], out.at[pl.ds(i * piece, piece)], out_sem.at[i]
        )
        store.start()
        stores.append(store)

    for copy in x_copies:
        copy.wait_send()
    for copy in l_copies:
        copy.wait_send()

    def sent(zz, q):
        @pl.when((zz <= z) & (z < lines - 1))
        def _():
            up(zz, q).wait_send()

        @pl.when((zz >= z) & (z > 0))
        def _():
            down(zz, q).wait_send()

        over(zz, q).wait_send()
        for yy in range(2):
            beside(at(zz, yy, c), q).wait_send()

    each(sent)
    for store in stores:
        store.wait()


def local(groups, terms, wave, left_env, right_env, right_sector, right_home):
    count, rows, cols = wave.shape
    held = left_env.shape[1]
    part = rows // terms
    lines = groups // 4
    chunks = 2 if terms == 2 else 1
    bf16 = jnp.bfloat16
    dma = pltpu.SemaphoreType.DMA
    any_spec = pl.BlockSpec(memory_space=pl.ANY)
    smem = pl.BlockSpec(memory_space=pltpu.SMEM)
    need = 2 * (
        groups * terms * held * part * cols + held * terms * rows * cols
        + count * rows * cols * (2 + terms)
    )
    return pl.pallas_call(
        functools.partial(kernel, (lines, terms, chunks)),
        out_shape=jax.ShapeDtypeStruct((count, rows, part), bf16),
        in_specs=[smem, smem, any_spec, any_spec, any_spec],
        out_specs=any_spec,
        scratch_shapes=[
            pltpu.VMEM((groups, terms, held, part, cols), bf16),
            pltpu.VMEM((held, terms, rows, cols), bf16),
            pltpu.VMEM((count, rows, cols), bf16),
            pltpu.VMEM((count, terms, rows, cols), bf16),
            pltpu.VMEM((count, rows, part), bf16),
            dma((PIECES,)),
            dma((2,)),
            dma((terms,)),
            dma((terms,)),
            dma((terms,)),
            dma((terms,)),
            dma((2, lines, chunks)),
            dma((lines, chunks)),
            dma((groups, chunks)),
            dma((groups, chunks)),
            dma((PIECES,)),
        ],
        compiler_params=pltpu.CompilerParams(
            collective_id=0, has_side_effects=True, vmem_limit_bytes=need + (8 << 20)
        ),
        cost_estimate=pl.CostEstimate(
            flops=4 * count * terms * rows * rows * cols,
            bytes_accessed=2 * count * rows * (cols + part),
            transcendentals=0,
        ),
    )(right_sector, right_home, wave, left_env, right_env)


def solution(mesh):
    groups, terms = mesh.shape["blk"], mesh.shape["mpo"]
    in_specs = (
        P("blk", None, None),
        P("mpo", "blk", None, None),
        P("mpo", "blk", None, None),
        P("blk", None),
        P(),
    )
    return jax.shard_map(
        functools.partial(local, groups, terms),
        mesh=mesh,
        in_specs=in_specs,
        out_specs=P("blk", None, "mpo"),
        check_vma=False,
    )
```

time: 153 us -> 41.4 us (0.27)
  waiting for transfers between devices: 117 us -> 0 us
  Pallas kernels: 0 us -> 33.7 us
  between operations: 13.4 us -> 0.02 us
  matrix products: 8.7 us -> 0 us
  other arithmetic: 4.28 us -> 0 us
  local copies, waits for them, and re-layouts: 9.55 us -> 7.49 us
    reduce_scatter x1 -> x0, waiting for transfers between devices: 76 us -> none  [local(): summed = lax.psum_scatter(terms, 'mpo', scatter_dimension=2, tiled=True)]
    all_gather x1 -> x0, waiting for transfers between devices: 40.2 us -> none  [local(): every_right = lax.all_gather(right_env[0], 'blk', axis=0, tiled=True)]
    pallas_call x0 -> x1, Pallas kernels: none -> 33.7 us  [local(): pl.pallas_call(functools.partial(kernel, (lines, terms, chunks)), out_sha...]
    gather x3 -> x0, local copies, waits for them, and re-layouts: 9.54 us -> none  [the longest x1 4.34 us: local(): picked = jnp.take(every_right, places, axis=0)]
    dot_general x1 -> x0, matrix products: 8.7 us -> none  [local(): jnp.einsum('bik,bjk->bij', left, picked, preferred_element_type=jnp.float32)]
    unnamed x4 -> x9, local copies, waits for them, and re-layouts: 0.01 us -> 5.1 us
    convert_element_type x1 -> x0, other arithmetic: 3.39 us -> none  [local(): return summed.astype(jnp.bfloat16)]
    pallas_call x0 -> x1, local copies, waits for them, and re-layouts: none -> 2.39 us  [local(): pl.pallas_call(functools.partial(kernel, (lines, terms, chunks)), out_sha...]
  transfers between devices with their start and end apart: 2 -> 0, of which waited for: 2 -> 0; matrix products, arithmetic and copies ran while one was open for 4% -> 0% of each run, Pallas kernels for 0% -> 0%
where the time goes in v1:
time: 41.4 us; the launch traced here: 41.2 us
  Pallas kernels  33.7 us (81%)
  local copies, waits for them, and re-layouts  7.49 us (18%)
    pallas_call x1, Pallas kernels, local(): pl.pallas_call(functools.partial(kernel, (lines, terms, chunks)), out_sha...  33.7 us
    unnamed x9, local copies, waits for them, and re-layouts  5.1 us
    pallas_call x1, local copies, waits for them, and re-layouts, local(): pl.pallas_call(functools.partial(kernel, (lines, terms, chunks)), out_sha...  2.39 us

profile of v1, /device:TPU:0, one launch (start us, length us, event | category | flops | bytes accessed | tf_op | source)
XLA Modules:
  0.0 41.2 jit_solution(15318626851837072907)
XLA Ops:
  0.0 0.8 %copy.6.sector = s32[96,1]{1,0:T(8,128)S(1)} copy(s32[96,1]{0,1:T(1,128)} %param.8) | data formatting | bytes 768 | tf_op args[3]
  0.8 0.0 copy-start
  0.8 1.9 %copy-done = bf16[96,128,128]{2,1,0:T(8,128)(2,1)S(1)} copy-done((bf16[96,128,128]{2,1,0:T(8,128)(2,1)S(1)}, bf16[96,128,128]{2,1,0:T(8,128)(2,1)}, u32[]{:S(2)}) %copy-start) | copy-done | bytes 3145752
  2.6 0.0 copy-start.1
  2.6 0.9 %copy-done.1 = bf16[1,4,128,128]{3,2,1,0:T(8,128)(2,1)S(1)} copy-done((bf16[1,4,128,128]{3,2,1,0:T(8,128)(2,1)S(1)}, bf16[1,4,128,128]{3,2,1,0:T(8,128)(2,1)}, u32[]{:S(2)}) %copy-start.1) | copy-done | bytes 131096
  3.5 0.0 copy-start.2
  3.5 0.9 %copy-done.2 = bf16[1,4,128,128]{3,2,1,0:T(8,128)(2,1)S(1)} copy-done((bf16[1,4,128,128]{3,2,1,0:T(8,128)(2,1)S(1)}, bf16[1,4,128,128]{3,2,1,0:T(8,128)(2,1)}, u32[]{:S(2)}) %copy-start.2) | copy-done | bytes 131096
  4.5 0.0 copy-start.3
  4.5 0.7 %copy-done.3 = s32[64]{0:T(128)S(1)} copy-done((s32[64]{0:T(128)S(1)}, s32[64]{0:T(128)}, u32[]{:S(2)}) %copy-start.3) | copy-done | bytes 280
  5.1 33.7 %shard_map.55 = bf16[96,128,64]{2,1,0:T(8,128)(2,1)S(1)} custom-call(s32[96,1]{1,0:T(8,128)S(1)} %copy.6.sector, s32[64]{0:T(128)S(1)} %copy-done.3, bf16[96,128,128]{2,1,0:T(8,128)(2,1)S(1)} %copy-done, bf16[1,4,128,128]{3,2,1,0:T(8,128)(2,1)S(1)} %copy-done.1, bf16[1,4,128,128]{3,2,1,0:T(8,128)(2,1)S(1)} %copy-done.2), custom_call_target="tpu_custom_call" | custom-call | flops 1610612736 | bytes 4718592 | tf_op jit(solution)/shard_map/pallas_call | solution.py:273
  38.8 2.4 %copy.7 = bf16[96,128,64]{1,2,0:T(8,128)(2,1)} copy(bf16[96,128,64]{2,1,0:T(8,128)(2,1)S(1)} %shard_map.55) | data formatting | bytes 3145728 | tf_op jit(solution)/shard_map/pallas_call | solution.py:273
Async XLA Ops:
  0.8 1.9 %copy-start = (bf16[96,128,128]{2,1,0:T(8,128)(2,1)S(1)}, bf16[96,128,128]{2,1,0:T(8,128)(2,1)}, u32[]{:S(2)}) copy-start(bf16[96,128,128]{2,1,0:T(8,128)(2,1)} %wave.1) | copy-start | bytes 9437188
  2.6 0.9 %copy-start.1 = (bf16[1,4,128,128]{3,2,1,0:T(8,128)(2,1)S(1)}, bf16[1,4,128,128]{3,2,1,0:T(8,128)(2,1)}, u32[]{:S(2)}) copy-start(bf16[1,4,128,128]{3,2,1,0:T(8,128)(2,1)} %lenv.1) | copy-start | bytes 393220
  3.5 0.9 %copy-start.2 = (bf16[1,4,128,128]{3,2,1,0:T(8,128)(2,1)S(1)}, bf16[1,4,128,128]{3,2,1,0:T(8,128)(2,1)}, u32[]{:S(2)}) copy-start(bf16[1,4,128,128]{3,2,1,0:T(8,128)(2,1)} %renv.1) | copy-start | bytes 393220
  4.5 0.7 %copy-start.3 = (s32[64]{0:T(128)S(1)}, s32[64]{0:T(128)}, u32[]{:S(2)}) copy-start(s32[64]{0:T(128)} %home.1) | copy-start | bytes 772

commit v2 on v1

--- a/solution.py
+++ b/solution.py
@@ -8,7 +8,7 @@
 from jax.sharding import PartitionSpec as P
 
 MESH = pl.DeviceIdType.MESH
-PIECES = 4
+PIECES = 8
 
 
 def kernel(
@@ -175,28 +175,32 @@
         def body(t, carry):
             j = i * piece + 2 * t
             a = j * held // count
-            stack = jnp.concatenate([lefts[a, w] for w in range(terms)], axis=0)
             pair = jnp.concatenate([blocks_in[j], blocks_in[j + 1]], axis=1)
-            both = jnp.dot(stack, pair, preferred_element_type=jnp.float32).astype(jnp.bfloat16)
             for w in range(terms):
-                left[j, w] = both[w * rows:(w + 1) * rows, :cols]
-                left[j + 1, w] = both[w * rows:(w + 1) * rows, cols:]
+                both = jnp.dot(lefts[a, w], pair, preferred_element_type=jnp.float32).astype(jnp.bfloat16)
+                left[j, w] = both[:, :cols]
+                left[j + 1, w] = both[:, cols:]
             return carry
 
-        lax.fori_loop(0, piece // 2, body, 0)
+        lax.fori_loop(0, piece // 2, body, 0, unroll=6)
 
     own_line()
+    hop(1)
     own_left.wait()
     for peer in peers:
         pltpu.make_async_copy(lenv.at[0], lefts.at[:, peer], l_recv.at[peer]).wait()
-    first(0)
-    for h in range(1, lines):
+    done = 0
+    for h in range(2, lines):
+        if done < PIECES:
+            first(done)
+            done += 1
         hop(h)
-        cross(h - 1)
-        if h < PIECES - 1:
-            first(h)
-    cross(lines - 1)
-    for i in range(min(lines, PIECES - 1), PIECES):
+    for h in range(lines):
+        if done < PIECES:
+            first(done)
+            done += 1
+        cross(h)
+    for i in range(done, PIECES):
         first(i)
 
     def each(body):
@@ -217,16 +221,16 @@
     for i in range(PIECES):
 
         def second(j, carry):
-            place = home[sector[j, 0]]
+            place = home[sector[0, j]]
             source, slot = place // held, place % held
             mine = jnp.concatenate([left[j, w] for w in range(terms)], axis=1)
             right = jnp.concatenate([rights[source, w, slot] for w in range(terms)], axis=1)
             result[j] = lax.dot_general(
-                mine, right, (((1,), (1,)), ((), ())), preferred_element_type=jnp.float32
+                right, mine, (((1,), (1,)), ((), ())), preferred_element_type=jnp.float32
             ).astype(jnp.bfloat16)
             return carry
 
-        lax.fori_loop(i * piece, (i + 1) * piece, second, 0, unroll=4)
+        lax.fori_loop(i * piece, (i + 1) * piece, second, 0, unroll=12)
         store = pltpu.make_async_copy(
             result.at[pl.ds(i * piece, piece)], out.at[pl.ds(i * piece, piece)], out_sem.at[i]
         )
@@ -266,13 +270,9 @@
     dma = pltpu.SemaphoreType.DMA
     any_spec = pl.BlockSpec(memory_space=pl.ANY)
     smem = pl.BlockSpec(memory_space=pltpu.SMEM)
-    need = 2 * (
-        groups * terms * held * part * cols + held * terms * rows * cols
-        + count * rows * cols * (2 + terms)
-    )
-    return pl.pallas_call(
+    product = pl.pallas_call(
         functools.partial(kernel, (lines, terms, chunks)),
-        out_shape=jax.ShapeDtypeStruct((count, rows, part), bf16),
+        out_shape=jax.ShapeDtypeStruct((count, part, rows), bf16),
         in_specs=[smem, smem, any_spec, any_spec, any_spec],
         out_specs=any_spec,
         scratch_shapes=[
@@ -280,7 +280,7 @@
             pltpu.VMEM((held, terms, rows, cols), bf16),
             pltpu.VMEM((count, rows, cols), bf16),
             pltpu.VMEM((count, terms, rows, cols), bf16),
-            pltpu.VMEM((count, rows, part), bf16),
+            pltpu.VMEM((count, part, rows), bf16),
             dma((PIECES,)),
             dma((2,)),
             dma((terms,)),
@@ -294,14 +294,15 @@
             dma((PIECES,)),
         ],
         compiler_params=pltpu.CompilerParams(
-            collective_id=0, has_side_effects=True, vmem_limit_bytes=need + (8 << 20)
+            collective_id=0, has_side_effects=True, vmem_limit_bytes=60 << 20
         ),
         cost_estimate=pl.CostEstimate(
             flops=4 * count * terms * rows * rows * cols,
             bytes_accessed=2 * count * rows * (cols + part),
             transcendentals=0,
         ),
-    )(right_sector, right_home, wave, left_env, right_env)
+    )(right_sector.reshape(1, count), right_home, wave, left_env, right_env)
+    return jnp.swapaxes(product, 1, 2)
 
 
 def solution(mesh):

time: 41.4 us -> 30.5 us (0.74)
  Pallas kernels: 33.7 us -> 27.6 us
  local copies, waits for them, and re-layouts: 7.49 us -> 2.67 us
    pallas_call x1, Pallas kernels: 33.7 us -> 27.6 us  [local(): pl.pallas_call(functools.partial(kernel, (lines, terms, chunks)), out_sha...]
    unnamed x9 -> x1, local copies, waits for them, and re-layouts: 5.1 us -> 2.67 us
    pallas_call x1 -> x0, local copies, waits for them, and re-layouts: 2.39 us -> none  [local(): pl.pallas_call(functools.partial(kernel, (lines, terms, chunks)), out_sha...]
where the time goes in v2:
time: 30.5 us; the launch traced here: 30.3 us
  Pallas kernels  27.6 us (90%)
  local copies, waits for them, and re-layouts  2.67 us (9%)
    pallas_call x1, Pallas kernels, local(): pl.pallas_call(functools.partial(kernel, (lines, terms, chunks)), out_sha...  27.6 us
    unnamed x1, local copies, waits for them, and re-layouts  2.67 us

profile of v2, /device:TPU:0, one launch (start us, length us, event | category | flops | bytes accessed | tf_op | source)
XLA Modules:
  0.0 30.3 jit_solution(8910608213330338924)
XLA Ops:
  0.0 27.6 %shard_map.55 = bf16[96,64,128]{2,1,0:T(8,128)(2,1)} custom-call(s32[1,96]{1,0:T(1,128)} %bitcast.3, s32[64]{0:T(128)} %home.1, bf16[96,128,128]{2,1,0:T(8,128)(2,1)} %wave.1, bf16[1,4,128,128]{3,2,1,0:T(8,128)(2,1)} %lenv.1, bf16[1,4,128,128]{3,2,1,0:T(8,128)(2,1)} %renv.1), custom_call_target="tpu_custom_call" | custom-call | flops 1610612736 | bytes 4718592 | tf_op jit(solution)/shard_map/pallas_call | solution.py:273
  27.6 2.7 %copy.7 = bf16[96,128,64]{1,2,0:T(8,128)(2,1)} copy(bf16[96,128,64]{1,2,0:T(8,128)(2,1)} %bitcast.2) | data formatting | bytes 3145728

commit v3 on v2

--- a/solution.py
+++ b/solution.py
@@ -83,8 +83,6 @@
     ]
     for copy in x_copies:
         copy.start()
-    for copy in l_copies:
-        copy.start()
 
     def unit(bb, q):
         return rights.at[bb, pl.ds(q * per, per)]
@@ -108,6 +106,7 @@
         return to(bb, q, c_send.at[bb, q], sibling)
 
     def spread(zz, q, upward, downward):
+        over(zz, q).start()
         if upward:
 
             @pl.when(z < lines - 1)
@@ -120,7 +119,6 @@
             def _():
                 down(zz, q).start()
 
-        over(zz, q).start()
         beside(at(zz, y, c), q).start()
 
     order = [m, 1 - m] if chunks == 2 else [0]
@@ -185,6 +183,8 @@
         lax.fori_loop(0, piece // 2, body, 0, unroll=6)
 
     own_line()
+    for copy in l_copies:
+        copy.start()
     hop(1)
     own_left.wait()
     for peer in peers:

time: 30.5 us -> 30.1 us (0.987)
  Pallas kernels: 27.6 us -> 27.2 us
    pallas_call x1, Pallas kernels: 27.6 us -> 27.2 us  [local(): pl.pallas_call(functools.partial(kernel, (lines, terms, chunks)), out_sha...]
where the time goes in v3:
time: 30.1 us; the launch traced here: 29.9 us
  Pallas kernels  27.2 us (90%)
  local copies, waits for them, and re-layouts  2.67 us (9%)
    pallas_call x1, Pallas kernels, local(): pl.pallas_call(functools.partial(kernel, (lines, terms, chunks)), out_sha...  27.2 us
    unnamed x1, local copies, waits for them, and re-layouts  2.67 us

profile of v3, /device:TPU:0, one launch (start us, length us, event | category | flops | bytes accessed | tf_op | source)
XLA Modules:
  0.0 29.9 jit_solution(131852914422611722)
XLA Ops:
  0.0 27.2 %shard_map.55 = bf16[96,64,128]{2,1,0:T(8,128)(2,1)} custom-call(s32[1,96]{1,0:T(1,128)} %bitcast.3, s32[64]{0:T(128)} %home.1, bf16[96,128,128]{2,1,0:T(8,128)(2,1)} %wave.1, bf16[1,4,128,128]{3,2,1,0:T(8,128)(2,1)} %lenv.1, bf16[1,4,128,128]{3,2,1,0:T(8,128)(2,1)} %renv.1), custom_call_target="tpu_custom_call" | custom-call | flops 1610612736 | bytes 4718592 | tf_op jit(solution)/shard_map/pallas_call | solution.py:273
  27.2 2.7 %copy.7 = bf16[96,128,64]{1,2,0:T(8,128)(2,1)} copy(bf16[96,128,64]{1,2,0:T(8,128)(2,1)} %bitcast.2) | data formatting | bytes 3145728
